TPU v7x, 32 devices: a whole 2x2x4 slice. The times are simulated.
32 devices in a mesh: vrow: 16 (over z, y, core), vcol: 2 (over x).
Axes of the slice: x: 2, y: 2, z: 4, core: 2. Of those that a mesh axis runs over, the one named last changes fastest.
Arguments:
- pairs: int32 [64, 2], replicated, may hold values from 0 to 119, as said below
- offsets: int32 [2, 2], replicated, may hold values from 0 to 1016, as said below
- amplitudes: bfloat16 [64, 1024, 1024], P(None, 'vrow', 'vcol'), may hold values from -0.59765625 to 0.59765625
- slabs: bfloat16 [2, 2, 1024, 8, 2304], P(None, None, ('vrow', 'vcol')), may hold values from -0.86328125 to 0.86328125
Outputs:
- residual: float32 [64, 1024, 1024], P(None, 'vrow', 'vcol')
Inputs may be any that keep to these rules, and one draw needn't show every extreme that they name: `pairs`: each row is an occupied pair i <= j; some rows have i = j. `offsets`: every offset is a multiple of 8.
All inputs are finite; a program needn't handle non-finite values.
Results may differ from a plain program's by a relative error of at most 0.0003.
Values may be sent and summed in bfloat16 or wider, within the bound.
A program may use at most 192 MiB of HBM per device.

v0:
```python
import jax
import jax.numpy as jnp
from jax import lax
from jax.sharding import PartitionSpec as P

BLK = 8
P_SIZE = 64
STEPS = 2


def broadcast(block, axis, holder):
    block = jnp.where(lax.axis_index(axis) == holder, block, jnp.zeros_like(block))
    return lax.psum(block, axis)


def ladder_part(rows, upper, lower, piece):
    depth = rows.shape[-1]
    count_a = rows.shape[2]
    count_b = piece.shape[2]
    rows_c = rows[0, 0].reshape(count_a * BLK, depth)
    rows_d = rows[0, 1].reshape(count_a * BLK, depth)
    piece_c = piece[0, 0].reshape(count_b * BLK, depth)
    piece_d = piece[0, 1].reshape(count_b * BLK, depth)
    direct = lax.dot_general(
        rows_c, piece_d, (((1,), (1,)), ((), ())), preferred_element_type=jnp.float32
    ).reshape(count_a, BLK, count_b, BLK)
    swapped = lax.dot_general(
        rows_d, piece_c, (((1,), (1,)), ((), ())), preferred_element_type=jnp.float32
    ).reshape(count_a, BLK, count_b, BLK)
    term = jnp.einsum("acbd,pcd->pab", direct, upper[0], precision=lax.Precision.HIGHEST)
    term = term + jnp.einsum("adbc,pcd->pab", swapped, lower[0], precision=lax.Precision.HIGHEST)
    term = term[None]
    return term


def on_device(pairs, offsets, amplitudes, slabs):
    row_count = lax.axis_size("vrow")
    col_count = lax.axis_size("vcol")
    rows_loc = amplitudes.shape[1]
    cols_loc = amplitudes.shape[2]
    offdiag = (pairs[:, 0] != pairs[:, 1]).astype(jnp.float32)
    zero = jnp.zeros((), jnp.int32)
    upper_list = []
    lower_list = []
    for k in range(STEPS):
        first = offsets[k, 0]
        second = offsets[k, 1]
        own_forward = lax.dynamic_slice(
            amplitudes, (zero, first % rows_loc, second % cols_loc), (P_SIZE, BLK, BLK)
        )
        own_mirror = lax.dynamic_slice(
            amplitudes, (zero, second % rows_loc, first % cols_loc), (P_SIZE, BLK, BLK)
        )
        root_forward = first // rows_loc * col_count + second // cols_loc
        root_mirror = second // rows_loc * col_count + first // cols_loc
        forward = broadcast(own_forward, ("vrow", "vcol"), root_forward).astype(jnp.float32)
        mirror_raw = broadcast(own_mirror, ("vrow", "vcol"), root_mirror).astype(jnp.float32)
        mirror = jnp.transpose(mirror_raw, (0, 2, 1))
        plus = 0.5 * (forward + mirror)
        minus = 0.5 * (forward - mirror) * offdiag[:, None, None]
        upper_list.append(plus + minus)
        lower_list.append(plus - minus)
    results = None
    for k in range(STEPS):
        rows = lax.all_gather(slabs[k], "vcol", axis=1, tiled=True)

        def single(piece, start, rows=rows, k=k):
            return ladder_part(rows[None], upper_list[k][None], lower_list[k][None], piece[None])

        term = single(lax.all_gather(slabs[k], "vrow", axis=1, tiled=True), jnp.int32(0))
        results = term if results is None else results + term
    groups = row_count // col_count
    inner = cols_loc // row_count
    shaped = results[0].reshape(P_SIZE, rows_loc, col_count, groups, 1, inner)
    moved = lax.all_to_all(shaped, "vcol", split_axis=2, concat_axis=4, tiled=True)
    combined = moved.reshape(P_SIZE, rows_loc, cols_loc)
    return combined


def solution(mesh):
    in_specs = (P(), P(), P(None, "vrow", "vcol"), P(None, None, ("vrow", "vcol"), None, None))
    out_specs = P(None, "vrow", "vcol")
    return jax.shard_map(
        on_device, mesh=mesh, in_specs=in_specs, out_specs=out_specs, check_vma=False
    )
```

profile of v0, /device:TPU:9, one launch (start us, length us, event | category | flops | bytes accessed | tf_op | source)
XLA Modules:
  0.0 820.8 jit_solution(13974830813240165925)
XLA Ops:
  6.5 2.7 fusion.52
  9.2 1.9 copy.94
  11.2 1.8 copy.91
  13.1 0.7 all-gather.15.cloned.1.call-update
  14.4 0.7 fusion.53
  25.0 1.9 constant_dynamic-slice_fusion.3
  27.5 42.4 %all-reduce = (bf16[64,8,8]{0,2,1:T(8,128)(2,1)}, bf16[64,8,8]{0,1,2:T(8,128)(2,1)S(1)}, bf16[64,8,8]{0,2,1:T(8,128)(2,1)}, bf16[64,8,8]{0,1,2:T(8,128)(2,1)}) all-reduce(bf16[64,8,8]{0,2,1:T(8,128)(2,1)S(1)} %get-tuple-element.23, bf16[64,8,8]{0,1,2:T(8,128)(2,1)S(1)} %get-tuple-element.25, ...), channel_id=1, replica_groups=mesh['vrow'=16,'vcol'=2] {'vrow','vcol'}, use_global_device_ids=true, to_apply=%region_3.4 | all-reduce | flops 16384 | bytes 65536 | tf_op jit(solution)/shard_map/psum | solution.py:13
  69.9 0.6 convert_element_type.14
  70.5 0.5 fusion.47
  71.1 5.4 all-gather.13.cloned.1.call-done
  76.5 4.2 slice_bitcast_fusion.9
  80.7 60.1 %all-gather.9.cloned.1.call-done = bf16[1,2,64,8,2304]{4,2,3,1,0:T(8,128)(2,1)} async-done(((bf16[1,2,32,8,2304]{4,2,3,1,0:T(8,128)(2,1)}), bf16[1,2,64,8,2304]{4,2,3,1,0:T(8,128)(2,1)}) %all-gather.9.cloned.1.call-update) | async-done | bytes 4718608 | tf_op jit(solution)/shard_map/all_gather | solution.py:65
  140.7 4.9 slice_bitcast_fusion.11
  145.7 184.9 %all-gather.15.cloned.1.call-done = bf16[1,2,512,8,2304]{4,2,3,1,0:T(8,128)(2,1)} async-done(((bf16[1,2,32,8,2304]{4,2,3,1,0:T(8,128)(2,1)}), bf16[1,2,512,8,2304]{4,2,3,1,0:T(8,128)(2,1)}) %all-gather.15.cloned.1.call-update) | async-done | bytes 37748752 | tf_op jit(solution)/shard_map/all_gather | solution.py:70
  330.6 16.4 %fusion = f32[64,8,512,8]{2,1,3,0:T(8,128)} fusion(bf16[1,2,512,8,2304]{4,2,3,1,0:T(8,128)(2,1)} %all-gather.15.cloned.1.call-done, bf16[64,8,2304,1]{2,0,1,3:T(8,128)(2,1)S(1)} %get-tuple-element.14), kind=kOutput, calls=%fused_computation.1 | convolution fusion | flops 9663676416 | bytes 29622272 | tf_op jit(solution)/shard_map/dot_general | solution.py:27
  347.0 12.0 %fusion.19 = f32[64,64,512,1]{2,0,3,1:T(8,128)} fusion(f32[64,8,512,8]{2,1,3,0:T(8,128)} %fusion, bf16[64,8,8]{0,2,1:T(8,128)(2,1)S(1)} %copy-done.9, f32[64,8,8]{0,1,2:T(8,128)S(1)} %copy-done.3, f32[64]{0:T(128)S(1)} %copy-done.11), kind=kOutput, calls=%fused_computation.31 | convolution fusion | flops 1610637312 | bytes 16802048 | tf_op jit(solution)/shard_map/adbc,pcd->pab/dot_general | solution.py:31
  359.0 16.9 %fusion.1 = f32[64,8,512,8]{2,1,3,0:T(8,128)} fusion(bf16[1,2,512,8,2304]{4,2,3,1,0:T(8,128)(2,1)} %all-gather.15.cloned.1.call-done, bf16[64,8,2304,1]{2,0,1,3:T(8,128)(2,1)S(1)} %copy-done.2), kind=kOutput, calls=%fused_computation.3 | convolution fusion | flops 9663676416 | bytes 29622272 | tf_op jit(solution)/shard_map/dot_general | solution.py:24
  376.0 15.5 %fusion.5 = f32[64,64,512,1]{2,0,3,1:T(8,128)} fusion(f32[64,8,512,8]{2,1,3,0:T(8,128)} %fusion.1, bf16[64,8,8]{0,2,1:T(8,128)(2,1)S(1)} %copy-done.10, f32[64,8,8]{0,1,2:T(8,128)S(1)} %copy-done.4, f32[64]{0:T(128)S(1)} %copy-done.12), kind=kOutput, calls=%fused_computation.11 | convolution fusion | flops 1610637312 | bytes 16802048 | tf_op jit(solution)/shard_map/acbd,pcd->pab/dot_general | solution.py:30
  391.5 128.3 %all-gather.11.cloned.1.call-done = bf16[1,2,512,8,2304]{4,2,3,1,0:T(8,128)(2,1)} async-done(((bf16[1,2,32,8,2304]{4,2,3,1,0:T(8,128)(2,1)}), bf16[1,2,512,8,2304]{4,2,3,1,0:T(8,128)(2,1)}) %all-gather.11.cloned.1.call-update) | async-done | bytes 37748752 | tf_op jit(solution)/shard_map/all_gather | solution.py:70
  519.8 16.8 %fusion.2 = f32[64,8,512,8]{2,1,3,0:T(8,128)} fusion(bf16[1,2,512,8,2304]{4,2,3,1,0:T(8,128)(2,1)} %all-gather.11.cloned.1.call-done, bf16[64,8,2304,1]{2,0,1,3:T(8,128)(2,1)S(1)} %copy-done.1), kind=kOutput, calls=%fused_computation.5 | convolution fusion | flops 9663676416 | bytes 29622272 | tf_op jit(solution)/shard_map/dot_general | solution.py:27
  536.6 11.8 %fusion.22 = f32[64,64,512,1]{2,0,3,1:T(8,128)} fusion(f32[64,8,512,8]{2,1,3,0:T(8,128)} %fusion.2, bf16[64,8,8]{0,2,1:T(8,128)(2,1)S(1)} %copy-done.5, f32[64]{0:T(128)S(1)} %copy-done.13, bf16[64,8,8]{0,1,2:T(8,128)(2,1)S(1)} %copy-done.7), kind=kOutput, calls=%fused_computation.34 | convolution fusion | flops 1610641408 | bytes 16793856 | tf_op jit(solution)/shard_map/adbc,pcd->pab/dot_general | solution.py:31
  548.4 16.5 %fusion.3 = f32[64,8,512,8]{2,1,3,0:T(8,128)} fusion(bf16[1,2,512,8,2304]{4,2,3,1,0:T(8,128)(2,1)} %all-gather.11.cloned.1.call-done, bf16[64,8,2304,1]{2,0,1,3:T(8,128)(2,1)S(1)} %copy-done), kind=kOutput, calls=%fused_computation.7 | convolution fusion | flops 9663676416 | bytes 29622272 | tf_op jit(solution)/shard_map/dot_general | solution.py:24
  565.0 20.4 %fusion.4 = f32[64,64,512]{2,0,1:T(8,128)} fusion(f32[64,64,512,1]{2,0,3,1:T(8,128)} %fusion.19, f32[64,64,512,1]{2,0,3,1:T(8,128)} %fusion.5, f32[64,64,512,1]{2,0,3,1:T(8,128)} %fusion.22, f32[64,8,512,8]{2,1,3,0:T(8,128)} %fusion.3, bf16[64,8,8]{0,2,1:T(8,128)(2,1)S(1)} %copy-done.6, f32[64]{0:T(128)S(1)} %copy-done.14, bf16[64,8,8]{0,1,2:T(8,128)(2,1)S(1)} %copy-done.8), kind=kOutput, calls=%fused_computation.9 | convolution fusion | flops 1616932864 | bytes 41959680 | tf_op jit(solution)/shard_map/acbd,pcd->pab/dot_general | solution.py:30
  585.4 12.3 %copy.63 = f32[64,64,512]{1,2,0:T(8,128)} copy(f32[64,64,512]{2,0,1:T(8,128)} %fusion.4) | data formatting | bytes 16777216 | tf_op jit(solution)/shard_map/add | solution.py:71
  597.7 12.1 %copy.132 = f32[64,64,2,8,1,32]{1,5,3,0,4,2:T(8,128)} copy(f32[64,64,2,8,1,32]{1,5,3,2,0,4:T(8,128)} %bitcast.87) | data formatting | bytes 16777216 | tf_op jit(solution)/shard_map/reshape;squeeze | solution.py:74
  609.7 21.3 %reshape.65 = f32[2,1,1048576]{2,1,0:T(1,128)} reshape(f32[2,1,64,8,32,64]{5,4,3,2,1,0:T(8,128)} %bitcast.88) | data formatting | bytes 16777216
  631.0 103.2 %all_to_all.15 = f32[2,1,1048576]{2,1,0:T(1,128)} all-to-all(f32[2,1,1048576]{2,1,0:T(1,128)} %reshape.65), channel_id=1, replica_groups=mesh['vrow'=16,'vcol'=2] {'vcol'}, dimensions={0} | all-to-all | bytes 16777216 | tf_op jit(solution)/shard_map/all_to_all | solution.py:75
  734.8 31.1 %reduce = f32[2,1048576]{1,0:T(2,128)} reduce(f32[2,1,1048576]{2,1,0:T(1,128)} %all_to_all.15, f32[]{:T(128)} %broadcast.57), dimensions={1}, to_apply=%all_to_all.11.reduce_sub_computation | reduce | bytes 16777220 | tf_op jit(solution)/shard_map/all_to_all | solution.py:75
  766.0 21.3 %reshape.66 = f32[2,1,64,8,32,64]{5,4,3,2,1,0:T(8,128)} reshape(f32[2,1048576]{1,0:T(2,128)} %reduce) | data formatting | bytes 16777216
  787.3 7.1 bitcast_bitcast_fusion
  794.3 7.0 copy.65
  801.3 12.7 %copy.66 = f32[64,64,512]{2,1,0:T(8,128)} copy(f32[64,64,512]{1,2,0:T(8,128)} %bitcast.89) | data formatting | bytes 16777216 | tf_op jit(solution)/shard_map/reshape | solution.py:76
  (48 shorter events, 1.8 us)
Async XLA Ops:
  6.5 70.0 %all-gather.13.cloned.1.call-start = ((), (), s32[]{:S(2)}) async-start(), calls=%async_computation.3 | async-start | bytes 7077888 | tf_op jit(solution)/shard_map/all_gather | solution.py:65
  9.2 5.1 copy-start.15
  11.1 59.4 %copy-start.16 = (s32[64,2]{0,1:T(2,128)S(1)}, s32[64,2]{0,1:T(2,128)}, u32[]{:S(2)}) copy-start(s32[64,2]{0,1:T(2,128)} %param.4) | copy-start | bytes 1540
  11.1 129.6 %all-gather.9.cloned.1.call-start = ((), (), s32[]{:S(2)}) async-start(), calls=%async_computation.1 | async-start | bytes 7077888 | tf_op jit(solution)/shard_map/all_gather | solution.py:65
  13.0 317.5 %all-gather.15.cloned.1.call-start = ((), (), s32[]{:S(2)}) async-start(), calls=%async_computation.4 | async-start | bytes 40108032 | tf_op jit(solution)/shard_map/all_gather | solution.py:70
  13.8 506.0 %all-gather.11.cloned.1.call-start = ((), (), s32[]{:S(2)}) async-start(), calls=%async_computation.2 | async-start | bytes 40108032 | tf_op jit(solution)/shard_map/all_gather | solution.py:70
  330.6 16.4 %copy-start.3 = (f32[64,8,8]{0,1,2:T(8,128)S(1)}, f32[64,8,8]{0,1,2:T(8,128)}, u32[]{:S(2)}) copy-start(f32[64,8,8]{0,1,2:T(8,128)} %convert_element_type.14) | copy-start | bytes 49156
  330.6 16.4 %copy-start.9 = (bf16[64,8,8]{0,2,1:T(8,128)(2,1)S(1)}, bf16[64,8,8]{0,2,1:T(8,128)(2,1)}, u32[]{:S(2)}) copy-start(bf16[64,8,8]{0,2,1:T(8,128)(2,1)} %get-tuple-element.5) | copy-start | bytes 24580
  330.6 16.4 %copy-start.11 = (f32[64]{0:T(128)S(1)}, f32[64]{0:T(128)}, u32[]{:S(2)}) copy-start(f32[64]{0:T(128)} %fusion.47) | copy-start | bytes 772
  347.0 12.0 %copy-start.2 = (bf16[64,8,2304,1]{2,0,1,3:T(8,128)(2,1)S(1)}, bf16[64,8,2304,1]{2,0,1,3:T(8,128)(2,1)}, u32[]{:S(2)}) copy-start(bf16[64,8,2304,1]{2,0,1,3:T(8,128)(2,1)} %get-tuple-element.13) | copy-start | bytes 7077892
  359.0 17.0 %copy-start.4 = (f32[64,8,8]{0,1,2:T(8,128)S(1)}, f32[64,8,8]{0,1,2:T(8,128)}, u32[]{:S(2)}) copy-start(f32[64,8,8]{0,1,2:T(8,128)} %convert_element_type.14) | copy-start | bytes 49156
  359.0 17.0 %copy-start.10 = (bf16[64,8,8]{0,2,1:T(8,128)(2,1)S(1)}, bf16[64,8,8]{0,2,1:T(8,128)(2,1)}, u32[]{:S(2)}) copy-start(bf16[64,8,8]{0,2,1:T(8,128)(2,1)} %get-tuple-element.5) | copy-start | bytes 24580
  359.0 17.0 %copy-start.12 = (f32[64]{0:T(128)S(1)}, f32[64]{0:T(128)}, u32[]{:S(2)}) copy-start(f32[64]{0:T(128)} %fusion.47) | copy-start | bytes 772
  375.9 143.9 %copy-start.1 = (bf16[64,8,2304,1]{2,0,1,3:T(8,128)(2,1)S(1)}, bf16[64,8,2304,1]{2,0,1,3:T(8,128)(2,1)}, u32[]{:S(2)}) copy-start(bf16[64,8,2304,1]{2,0,1,3:T(8,128)(2,1)} %get-tuple-element.10) | copy-start | bytes 7077892
  519.8 16.8 %copy-start.5 = (bf16[64,8,8]{0,2,1:T(8,128)(2,1)S(1)}, bf16[64,8,8]{0,2,1:T(8,128)(2,1)}, u32[]{:S(2)}) copy-start(bf16[64,8,8]{0,2,1:T(8,128)(2,1)} %get-tuple-element.7) | copy-start | bytes 24580
  519.8 16.8 %copy-start.7 = (bf16[64,8,8]{0,1,2:T(8,128)(2,1)S(1)}, bf16[64,8,8]{0,1,2:T(8,128)(2,1)}, u32[]{:S(2)}) copy-start(bf16[64,8,8]{0,1,2:T(8,128)(2,1)} %get-tuple-element.8) | copy-start | bytes 24580
  519.8 16.8 %copy-start.13 = (f32[64]{0:T(128)S(1)}, f32[64]{0:T(128)}, u32[]{:S(2)}) copy-start(f32[64]{0:T(128)} %fusion.47) | copy-start | bytes 772
  536.6 11.8 %copy-start = (bf16[64,8,2304,1]{2,0,1,3:T(8,128)(2,1)S(1)}, bf16[64,8,2304,1]{2,0,1,3:T(8,128)(2,1)}, u32[]{:S(2)}) copy-start(bf16[64,8,2304,1]{2,0,1,3:T(8,128)(2,1)} %get-tuple-element.9) | copy-start | bytes 7077892
  548.4 16.6 %copy-start.6 = (bf16[64,8,8]{0,2,1:T(8,128)(2,1)S(1)}, bf16[64,8,8]{0,2,1:T(8,128)(2,1)}, u32[]{:S(2)}) copy-start(bf16[64,8,8]{0,2,1:T(8,128)(2,1)} %get-tuple-element.7) | copy-start | bytes 24580
  548.4 16.6 %copy-start.8 = (bf16[64,8,8]{0,1,2:T(8,128)(2,1)S(1)}, bf16[64,8,8]{0,1,2:T(8,128)(2,1)}, u32[]{:S(2)}) copy-start(bf16[64,8,8]{0,1,2:T(8,128)(2,1)} %get-tuple-element.8) | copy-start | bytes 24580
  548.4 16.6 %copy-start.14 = (f32[64]{0:T(128)S(1)}, f32[64]{0:T(128)}, u32[]{:S(2)}) copy-start(f32[64]{0:T(128)} %fusion.47) | copy-start | bytes 772
Sparse Core Ops, SparseCore 0:
  11.2 65.2 all-gather.12
  78.0 62.6 all-gather.8
  142.3 188.2 all-gather.14
  332.0 187.8 all-gather.10
where the time goes:
time: 826 us; the launch traced here: 821 us
  waiting for transfers between devices  380 us (46%)
  blocking collectives  146 us (18%)
  matrix products  126 us (15%)
  local copies, waits for them, and re-layouts  113 us (14%)
  other arithmetic  32.3 us (4%)
  between operations  23.6 us (3%)
    all_gather x2, waiting for transfers between devices, on_device(): lax.all_gather(slabs[k], 'vrow', axis=1, tiled=True)  313 us
    all_to_all x1, blocking collectives, on_device(): lax.all_to_all(shaped, 'vcol', split_axis=2, concat_axis=4, tiled=True)  103 us
    all_gather x2, waiting for transfers between devices, on_device(): rows = lax.all_gather(slabs[k], 'vcol', axis=1, tiled=True)  65.5 us
    unnamed x42, local copies, waits for them, and re-layouts  46.9 us
    psum x1, blocking collectives, broadcast(): return lax.psum(block, axis)  42.4 us
    dot_general x2, matrix products, ladder_part(): jnp.einsum('acbd,pcd->pab', direct, upper[0], precision=lax.Precision.HIG...  35.9 us
    dot_general x2, matrix products, ladder_part(): lax.dot_general(rows_c, piece_d, (((1,), (1,)), ((), ())), preferred_elem...  33.5 us
    dot_general x2, matrix products, ladder_part(): lax.dot_general(rows_d, piece_c, (((1,), (1,)), ((), ())), preferred_elem...  33.2 us
  transfers between devices with their start and end apart: 4, of which 4 were waited for; matrix products, arithmetic and copies ran while one was open for 9% of the time, Pallas kernels for 0%

commit v1 on v0

--- a/solution.py
+++ b/solution.py
@@ -1,6 +1,10 @@
+import functools
+
 import jax
 import jax.numpy as jnp
 from jax import lax
+from jax.experimental import pallas as pl
+from jax.experimental.pallas import tpu as pltpu
 from jax.sharding import PartitionSpec as P
 
 BLK = 8
@@ -33,8 +37,7 @@
     return term
 
 
-def on_device(pairs, offsets, amplitudes, slabs):
-    row_count = lax.axis_size("vrow")
+def blocks_of(pairs, offsets, amplitudes):
     col_count = lax.axis_size("vcol")
     rows_loc = amplitudes.shape[1]
     cols_loc = amplitudes.shape[2]
@@ -60,6 +63,15 @@
         minus = 0.5 * (forward - mirror) * offdiag[:, None, None]
         upper_list.append(plus + minus)
         lower_list.append(plus - minus)
+    return upper_list, lower_list
+
+
+def on_device(pairs, offsets, amplitudes, slabs):
+    row_count = lax.axis_size("vrow")
+    col_count = lax.axis_size("vcol")
+    rows_loc = amplitudes.shape[1]
+    cols_loc = amplitudes.shape[2]
+    upper_list, lower_list = blocks_of(pairs, offsets, amplitudes)
     results = None
     for k in range(STEPS):
         rows = lax.all_gather(slabs[k], "vcol", axis=1, tiled=True)
@@ -77,9 +89,241 @@
     return combined
 
 
+MESH = pl.DeviceIdType.MESH
+LANES = 128
+PAIRS = ((1, 4), (2, 5), (3, 6), (0, 7))
+BEHIND = (0, 1, 2, 3, 7)
+AHEAD = (0, 4, 5, 6, 7)
+FORWARD = ((0, 0), (0, 1), (1, 0), (1, 1), (2, 0), (2, 1), (3, 0))
+BACKWARD = ((0, 1), (0, 0), (1, 1), (1, 0), (2, 1), (2, 0), (3, 1))
+
+
+def ring_place(row):
+    y = lax.rem(row // 2, 2)
+    z = row // 4
+    return z + y * (7 - 2 * z)
+
+
+def ring_row(place, core):
+    y = place // 4
+    z = place + y * (7 - 2 * place)
+    return z * 4 + y * 2 + core
+
+
+def ring_kernel(
+    weights, natural, turned, gathered, mine, theirs,
+    rows, piece, factor, totals,
+    f_send, f_recv, b_send, b_recv, s_send, s_recv, a_send, a_recv, o_send, o_recv, l_sem, p_sem, t_sem,
+):
+    row = lax.axis_index("vrow")
+    col = lax.axis_index("vcol")
+    core = lax.rem(row, 2)
+    place = ring_place(row)
+    right = (ring_row(lax.rem(place + 1, 8), core), col)
+    left = (ring_row(lax.rem(place + 7, 8), core), col)
+    sibling = (row + 1 - 2 * core, col)
+    partner = (row, 1 - col)
+
+    barrier = pltpu.get_barrier_semaphore()
+    for other in (right, left, sibling, partner):
+        pl.semaphore_signal(barrier, inc=1, device_id=other, device_id_type=MESH)
+    pl.semaphore_wait(barrier, 4)
+
+    def remote(src, dst, send, recv, target):
+        return pltpu.make_async_remote_copy(
+            src_ref=src, dst_ref=dst, send_sem=send, recv_sem=recv, device_id=target, device_id_type=MESH
+        )
+
+    def hop(order, slots, send, recv, target, i):
+        step, k = order[i]
+        src = turned.at[k] if step == 0 else gathered.at[slots[step], core, k]
+        return remote(src, gathered.at[slots[step + 1], core, k], send.at[i], recv.at[i], target)
+
+    forward = [hop(FORWARD, BEHIND, f_send, f_recv, right, i) for i in range(7)]
+    backward = [hop(BACKWARD, AHEAD, b_send, b_recv, left, i) for i in range(7)]
+
+    def share(slot, k):
+        src = turned.at[k] if slot == 0 else gathered.at[slot, core, k]
+        return remote(src, gathered.at[slot, core, k], s_send.at[slot, k], s_recv.at[slot, k], sibling)
+
+    shares = {(slot, k): share(slot, k) for slot in range(8) for k in range(2)}
+    width = natural.shape[2]
+    a_copy = remote(natural, rows.at[:, :, pl.ds(col * width, width), :], a_send, a_recv, partner)
+    a_own = pltpu.make_async_copy(natural, rows.at[:, :, pl.ds(col * width, width), :], l_sem.at[0])
+    own = pltpu.make_async_copy(turned, gathered.at[0, core], l_sem.at[1])
+
+    for i in range(2):
+        forward[i].start()
+        backward[i].start()
+    a_copy.start()
+    own.start()
+    a_own.start()
+    for k in range(2):
+        shares[0, k].start()
+
+    outs = [remote(totals.at[u], theirs.at[u], o_send.at[u], o_recv.at[u], partner) for u in range(4)]
+    keeps = [pltpu.make_async_copy(totals.at[u], mine.at[u], t_sem.at[u]) for u in range(4)]
+    count = rows.shape[2] // BLK
+    shard = turned.shape[3]
+
+    def compute(u):
+        loads = []
+        for e, slot in enumerate(PAIRS[u]):
+            for c in range(2):
+                for k in range(2):
+                    dst = piece.at[k, :, :, pl.ds((e * 2 + c) * shard, shard), :]
+                    loads.append(pltpu.make_async_copy(gathered.at[slot, c, k], dst, p_sem.at[e, c, k]))
+        for load in loads:
+            load.start()
+        for load in loads:
+            load.wait()
+
+        def products(i, carry):
+            k = i // 8
+            t = lax.rem(i // 4, 2)
+            d = lax.rem(i, 4)
+            cols = piece[k, 1 - t, pl.ds(d * 2, 2)].reshape(2 * LANES, piece.shape[-1])
+            part = lax.dot_general(
+                rows[k, t], cols, (((1,), (1,)), ((), ())), preferred_element_type=jnp.float32
+            ).reshape(count, BLK, 2 * LANES)
+            part = jnp.concatenate([part[:, :, :LANES], part[:, :, LANES:]], axis=1)
+            high = part.astype(jnp.bfloat16)
+            low = (part - high.astype(jnp.float32)).astype(jnp.bfloat16)
+            at = k * 256 + t * 128 + d * 16
+            factor[:, pl.ds(pl.multiple_of(at, 16), 16), :] = high
+            factor[:, pl.ds(pl.multiple_of(at + 64, 16), 16), :] = low
+            return carry
+
+        lax.fori_loop(0, 16, products, 0)
+
+        def contract(a, carry):
+            res = jnp.dot(weights[...], factor[a], preferred_element_type=jnp.float32)
+            totals[u, pl.ds(a, P_SIZE, stride=count), :] = res[:P_SIZE] + res[P_SIZE:]
+            return carry
+
+        lax.fori_loop(0, count, contract, 0)
+        outs[u].start()
+        keeps[u].start()
+
+    def sibling_here(slots):
+        for slot in slots:
+            for k in range(2):
+                shares[slot, k].wait_recv()
+
+    for i in range(7):
+        forward[i].wait_recv()
+        if i + 2 < 7:
+            forward[i + 2].start()
+        step, k = FORWARD[i]
+        shares[BEHIND[step + 1], k].start()
+        backward[i].wait_recv()
+        if i + 2 < 7:
+            backward[i + 2].start()
+        step, k = BACKWARD[i]
+        shares[AHEAD[step + 1], k].start()
+        if i == 1:
+            a_own.wait()
+            a_copy.wait_recv()
+        if i in (1, 3, 5):
+            u = i // 2
+            sibling_here(PAIRS[u])
+            compute(u)
+    own.wait()
+    sibling_here(PAIRS[3])
+    compute(3)
+    for copy in forward + backward + list(shares.values()) + [a_copy]:
+        copy.wait_send()
+    for u in range(4):
+        keeps[u].wait()
+        outs[u].wait()
+
+
+def place_kernel(table, mine, theirs, out):
+    i = pl.program_id(0)
+    half = table[4 + i]
+    swap = table[8]
+    a = mine[0]
+    b = theirs[0]
+    first = jnp.where(swap == 0, a, b)
+    second = jnp.where(swap == 0, b, a)
+    first = jnp.where(half == 0, first[:, :, :64], first[:, :, 64:])
+    second = jnp.where(half == 0, second[:, :, :64], second[:, :, 64:])
+    out[...] = jnp.concatenate(
+        [first[:, :, :32], second[:, :, :32], first[:, :, 32:], second[:, :, 32:]], axis=-1
+    )
+
+
+def ladder_weights(pairs, offsets, amplitudes):
+    uppers, lowers = blocks_of(pairs, offsets, amplitudes)
+    parts = []
+    for k in range(STEPS):
+        up = jnp.transpose(uppers[k], (0, 2, 1)).reshape(P_SIZE, BLK * BLK)
+        low = lowers[k].reshape(P_SIZE, BLK * BLK)
+        parts.extend([up, up, low, low])
+    full = jnp.concatenate(parts, axis=1)
+    high = lax.reduce_precision(full, exponent_bits=8, mantissa_bits=7)
+    return jnp.concatenate([high, full - high], axis=0).astype(jnp.bfloat16)
+
+
+def on_plane(pairs, offsets, amplitudes, slabs):
+    shard, depth = slabs.shape[2], slabs.shape[4]
+    rows_loc, cols_loc = amplitudes.shape[1], amplitudes.shape[2]
+    weights = ladder_weights(pairs, offsets, amplitudes)
+    natural = slabs.reshape(STEPS, 2, shard * BLK, depth)
+    turned = jnp.swapaxes(slabs, 2, 3)
+    bf16, f32 = jnp.bfloat16, jnp.float32
+    dma = pltpu.SemaphoreType.DMA
+    anywhere = pl.BlockSpec(memory_space=pl.ANY)
+    _, mine, theirs = pl.pallas_call(
+        ring_kernel,
+        out_shape=(
+            jax.ShapeDtypeStruct((8, 2, STEPS, 2, BLK, shard, depth), bf16),
+            jax.ShapeDtypeStruct((4, P_SIZE * rows_loc, LANES), f32),
+            jax.ShapeDtypeStruct((4, P_SIZE * rows_loc, LANES), f32),
+        ),
+        in_specs=[pl.BlockSpec(memory_space=pltpu.VMEM), anywhere, anywhere],
+        out_specs=(anywhere, anywhere, anywhere),
+        scratch_shapes=[
+            pltpu.VMEM((STEPS, 2, rows_loc * BLK, depth), bf16),
+            pltpu.VMEM((STEPS, 2, BLK, LANES, depth), bf16),
+            pltpu.VMEM((rows_loc, STEPS * 256, LANES), bf16),
+            pltpu.VMEM((4, P_SIZE * rows_loc, LANES), f32),
+            dma((7,)), dma((7,)), dma((7,)), dma((7,)), dma((8, 2)), dma((8, 2)),
+            dma, dma, dma((4,)), dma((4,)), dma((2,)), dma((2, 2, 2)), dma((4,)),
+        ],
+        compiler_params=pltpu.CompilerParams(
+            collective_id=0, has_side_effects=True, vmem_limit_bytes=60 * 1024 * 1024
+        ),
+        name="ladder_ring",
+    )(weights, natural, turned)
+    row = lax.axis_index("vrow")
+    col = lax.axis_index("vcol")
+    chip = jnp.arange(4, dtype=jnp.int32)
+    z = 2 * col + chip // 2
+    y = chip % 2
+    rel = (z + y * (7 - 2 * z) - ring_place(row)) % 8
+    block = jnp.array([3, 0, 1, 2, 3, 2, 1, 0], jnp.int32)[rel]
+    half = jnp.array([0, 1, 1, 1, 1, 0, 0, 0], jnp.int32)[rel]
+    table = jnp.concatenate([block, half, col[None].astype(jnp.int32)])
+    chunk = 16
+    source = pl.BlockSpec((1, chunk, rows_loc, LANES), lambda i, j, t: (t[i], j, 0, 0))
+    return pl.pallas_call(
+        place_kernel,
+        grid_spec=pltpu.PrefetchScalarGridSpec(
+            num_scalar_prefetch=1,
+            grid=(4, P_SIZE // chunk),
+            in_specs=[source, source],
+            out_specs=pl.BlockSpec((chunk, rows_loc, LANES), lambda i, j, t: (j, 0, i)),
+        ),
+        out_shape=jax.ShapeDtypeStruct((P_SIZE, rows_loc, cols_loc), f32),
+        name="ladder_place",
+    )(table, mine.reshape(4, P_SIZE, rows_loc, LANES), theirs.reshape(4, P_SIZE, rows_loc, LANES))
+
+
 def solution(mesh):
     in_specs = (P(), P(), P(None, "vrow", "vcol"), P(None, None, ("vrow", "vcol"), None, None))
     out_specs = P(None, "vrow", "vcol")
+    on_slice = on_plane if (mesh.shape["vrow"], mesh.shape["vcol"]) == (16, 2) else on_device
     return jax.shard_map(
-        on_device, mesh=mesh, in_specs=in_specs, out_specs=out_specs, check_vma=False
+        on_slice, mesh=mesh, in_specs=in_specs, out_specs=out_specs, check_vma=False
     )

time: 826 us -> 533 us (0.65)
  Pallas kernels: 0 us -> 466 us
  waiting for transfers between devices: 380 us -> 0 us
  matrix products: 126 us -> 0 us
  blocking collectives: 146 us -> 40.4 us
  local copies, waits for them, and re-layouts: 113 us -> 12.5 us
  other arithmetic: 32.3 us -> 2.18 us
  between operations: 23.6 us -> 10.3 us
    pallas_call x0 -> x2, Pallas kernels: none -> 466 us  [the longest x1 446 us: on_plane(): pl.pallas_call(ring_kernel, out_shape=(jax.ShapeDtypeStruct((8, 2, STEPS,...]
    all_gather x4 -> x0, waiting for transfers between devices: 379 us -> none  [the longest x2 313 us: on_device(): lax.all_gather(slabs[k], 'vrow', axis=1, tiled=True)]
    dot_general x8 -> x0, matrix products: 126 us -> none  [the longest x2 35.9 us: ladder_part(): jnp.einsum('acbd,pcd->pab', direct, upper[0], precision=lax.Precision.HIG...]
    all_to_all x1 -> x0, blocking collectives: 103 us -> none  [on_device(): lax.all_to_all(shaped, 'vcol', split_axis=2, concat_axis=4, tiled=True)]
    unnamed x42 -> x5, local copies, waits for them, and re-layouts: 46.9 us -> 6.11 us
    all_to_all x1 -> x0, other arithmetic: 31.1 us -> none  [on_device(): lax.all_to_all(shaped, 'vcol', split_axis=2, concat_axis=4, tiled=True)]
    all_to_all x3 -> x0, local copies, waits for them, and re-layouts: 14.6 us -> none  [on_device(): lax.all_to_all(shaped, 'vcol', split_axis=2, concat_axis=4, tiled=True)]
    reshape x1 -> x4, local copies, waits for them, and re-layouts: 12.7 us -> 0.31 us  [the longest x2 0.16 us: ladder_weights(): up = jnp.transpose(uppers[k], (0, 2, 1)).reshape(P_SIZE, BLK * BLK)]
  transfers between devices with their start and end apart: 4 -> 0, of which waited for: 4 -> 0; matrix products, arithmetic and copies ran while one was open for 9% -> 0% of each run, Pallas kernels for 0% -> 0%
where the time goes in v1:
time: 533 us; the launch traced here: 532 us
  Pallas kernels  466 us (87%)
  blocking collectives  40.4 us (8%)
  local copies, waits for them, and re-layouts  12.5 us (2%)
  between operations  10.3 us (2%)
    pallas_call x1, Pallas kernels, on_plane(): pl.pallas_call(ring_kernel, out_shape=(jax.ShapeDtypeStruct((8, 2, STEPS,...  446 us
    psum x1, blocking collectives, broadcast(): return lax.psum(block, axis)  40.4 us
    pallas_call x1, Pallas kernels, on_plane(): pl.pallas_call(place_kernel, grid_spec=pltpu.PrefetchScalarGridSpec(num_s...  19.9 us

profile of v1, /device:TPU:9, one launch (start us, length us, event | category | flops | bytes accessed | tf_op | source)
XLA Modules:
  0.0 531.6 jit_solution(10344043193599869730)
XLA Ops:
  0.0 0.8 fusion.8
  0.8 1.5 fusion.11
  12.5 1.3 gather_fusion.1
  13.8 1.3 gather_fusion
  15.0 0.7 pad_add_fusion.table
  15.7 1.8 constant_dynamic-slice_fusion
  17.5 0.1 copy.37
  17.7 0.1 copy.35
  17.8 0.1 copy.34
  18.0 0.1 copy.36
  18.1 40.4 %all-reduce = (bf16[64,8,8]{0,2,1:T(8,128)(2,1)S(1)}, bf16[64,8,8]{0,2,1:T(8,128)(2,1)S(1)}, bf16[64,8,8]{0,1,2:T(8,128)(2,1)S(1)}, bf16[64,8,8]{0,2,1:T(8,128)(2,1)S(1)}) all-reduce(bf16[64,8,8]{0,2,1:T(8,128)(2,1)S(1)} %get-tuple-element.32, ...), channel_id=1, replica_groups=mesh['vrow'=16,'vcol'=2] {'vrow','vcol'}, use_global_device_ids=true, to_apply=%region_1.2 | all-reduce | flops 16384 | bytes 65536 | tf_op jit(solution)/shard_map/psum | solution.py:17
  58.6 0.1 copy.31
  58.7 0.1 copy.29
  58.8 0.1 copy.25
  58.9 0.1 copy.27
  59.0 0.1 concatenate.11
  59.1 0.7 pad_maximum_fusion.weights
  59.8 5.6 %copy.53 = bf16[2,2,32,8,2304]{4,2,3,1,0:T(8,128)(2,1)} copy(bf16[2,2,32,8,2304]{4,3,2,1,0:T(8,128)(2,1)} %param.9) | data formatting | bytes 9437184 | tf_op args[3]
  65.3 446.4 %ladder_ring.1 = (bf16[8,2,2,2,8,32,2304]{6,5,4,3,2,1,0:T(8,128)(2,1)}, f32[4,4096,128]{2,1,0:T(8,128)}, f32[4,4096,128]{2,1,0:T(8,128)}) custom-call(bf16[128,512]{1,0:T(8,128)(2,1)} %pad_maximum_fusion.weights, bf16[2,2,256,2304]{3,2,1,0:T(8,128)(2,1)} %bitcast.33, bf16[2,2,8,32,2304]{4,3,2,1,0:T(8,128)(2,1)} %bitcast.34), custom_call_target="tpu_custom_call" | custom-call | tf_op jit(solution)/shard_map/ladder_ring/pallas_call | solution.py:277
  511.8 19.9 %ladder_place.1 = f32[64,64,512]{2,1,0:T(8,128)} custom-call(s32[9]{0:T(128)} %pad_add_fusion.table, f32[4,64,64,128]{3,2,1,0:T(8,128)} %bitcast.35, f32[4,64,64,128]{3,2,1,0:T(8,128)} %bitcast.36), custom_call_target="tpu_custom_call" | custom-call | tf_op jit(solution)/shard_map/ladder_place/pallas_call | solution.py:310
  (10 shorter events, 0.1 us)

commit v2 on v1

--- a/solution.py
+++ b/solution.py
@@ -111,8 +111,8 @@
 
 
 def ring_kernel(
-    weights, natural, turned, gathered, mine, theirs,
-    rows, piece, factor, totals,
+    own_blocks, sides, natural, turned, gathered, mine, theirs,
+    rows, piece, factor, totals, weights, sums, came, packed, x_send, x_recv,
     f_send, f_recv, b_send, b_recv, s_send, s_recv, a_send, a_recv, o_send, o_recv, l_sem, p_sem, t_sem,
 ):
     row = lax.axis_index("vrow")
@@ -125,9 +125,12 @@
     partner = (row, 1 - col)
 
     barrier = pltpu.get_barrier_semaphore()
-    for other in (right, left, sibling, partner):
+    flips = [sibling, partner]
+    for bit in (2, 4, 8):
+        flips.append((row + bit - 2 * bit * lax.rem(row // bit, 2), col))
+    for other in [right, left] + flips:
         pl.semaphore_signal(barrier, inc=1, device_id=other, device_id_type=MESH)
-    pl.semaphore_wait(barrier, 4)
+    pl.semaphore_wait(barrier, 7)
 
     def remote(src, dst, send, recv, target):
         return pltpu.make_async_remote_copy(
@@ -151,6 +154,13 @@
     a_copy = remote(natural, rows.at[:, :, pl.ds(col * width, width), :], a_send, a_recv, partner)
     a_own = pltpu.make_async_copy(natural, rows.at[:, :, pl.ds(col * width, width), :], l_sem.at[0])
     own = pltpu.make_async_copy(turned, gathered.at[0, core], l_sem.at[1])
+
+    sums[0] = own_blocks[...]
+    for i, other in enumerate(flips):
+        swap = remote(sums.at[i], came.at[i], x_send.at[i], x_recv.at[i], other)
+        swap.start()
+        swap.wait()
+        sums[i + 1] = sums[i] + came[i]
 
     for i in range(2):
         forward[i].start()
@@ -161,7 +171,16 @@
     for k in range(2):
         shares[0, k].start()
 
-    outs = [remote(totals.at[u], theirs.at[u], o_send.at[u], o_recv.at[u], partner) for u in range(4)]
+    ahead = sums[5, 0].astype(jnp.float32)
+    mirror = sums[5, 1].astype(jnp.float32)
+    full = 0.5 * (ahead + mirror) + 0.5 * (ahead - mirror) * sides[...]
+    high = full.astype(jnp.bfloat16)
+    weights[:P_SIZE] = high
+    weights[P_SIZE:] = (full - high.astype(jnp.float32)).astype(jnp.bfloat16)
+
+    outs = [remote(totals.at[u], theirs.at[u], o_send.at[u], o_recv.at[u], partner) for u in range(3)]
+    outs.append(remote(packed, theirs.at[3, pl.ds(0, packed.shape[0])], o_send.at[3], o_recv.at[3], partner))
+    send_last = row // 8 == col
     keeps = [pltpu.make_async_copy(totals.at[u], mine.at[u], t_sem.at[u]) for u in range(4)]
     count = rows.shape[2] // BLK
     shard = turned.shape[3]
@@ -198,7 +217,15 @@
 
         def contract(a, carry):
             res = jnp.dot(weights[...], factor[a], preferred_element_type=jnp.float32)
-            totals[u, pl.ds(a, P_SIZE, stride=count), :] = res[:P_SIZE] + res[P_SIZE:]
+            res = res[:P_SIZE] + res[P_SIZE:]
+            totals[u, pl.ds(a, P_SIZE, stride=count), :] = res
+            if u == 3:
+                moved = pltpu.roll(res, 64, 1)
+                half = P_SIZE // 2
+                low = lax.broadcasted_iota(jnp.int32, (half, LANES), 1) < 64
+                opposite = jnp.where(low, moved[:half], res[half:])
+                near = jnp.where(low, res[:half], moved[half:])
+                packed[pl.ds(a, half, stride=count), :] = jnp.where(send_last, opposite, near)
             return carry
 
         lax.fori_loop(0, count, contract, 0)
@@ -241,34 +268,51 @@
 def place_kernel(table, mine, theirs, out):
     i = pl.program_id(0)
     half = table[4 + i]
+    other_half = jnp.where(table[i] == 3, pl.program_id(1) // 2, half)
     swap = table[8]
     a = mine[0]
     b = theirs[0]
+    a = jnp.where(half == 0, a[:, :, :64], a[:, :, 64:])
+    b = jnp.where(other_half == 0, b[:, :, :64], b[:, :, 64:])
     first = jnp.where(swap == 0, a, b)
     second = jnp.where(swap == 0, b, a)
-    first = jnp.where(half == 0, first[:, :, :64], first[:, :, 64:])
-    second = jnp.where(half == 0, second[:, :, :64], second[:, :, 64:])
     out[...] = jnp.concatenate(
         [first[:, :, :32], second[:, :, :32], first[:, :, 32:], second[:, :, 32:]], axis=-1
     )
 
 
-def ladder_weights(pairs, offsets, amplitudes):
-    uppers, lowers = blocks_of(pairs, offsets, amplitudes)
-    parts = []
+def ladder_blocks(pairs, offsets, amplitudes):
+    rows_loc, cols_loc = amplitudes.shape[1], amplitudes.shape[2]
+    here = lax.axis_index(("vrow", "vcol"))
+    col_count = lax.axis_size("vcol")
+    zero = jnp.zeros((), jnp.int32)
+
+    def own(first, second):
+        block = lax.dynamic_slice(
+            amplitudes, (zero, first % rows_loc, second % cols_loc), (P_SIZE, BLK, BLK)
+        )
+        root = first // rows_loc * col_count + second // cols_loc
+        return jnp.where(here == root, block, jnp.zeros_like(block))
+
+    def both(block_cd):
+        cd = block_cd.reshape(P_SIZE, BLK * BLK)
+        dc = jnp.transpose(block_cd, (0, 2, 1)).reshape(P_SIZE, BLK * BLK)
+        return [dc, dc, cd, cd]
+
+    ahead, mirror = [], []
     for k in range(STEPS):
-        up = jnp.transpose(uppers[k], (0, 2, 1)).reshape(P_SIZE, BLK * BLK)
-        low = lowers[k].reshape(P_SIZE, BLK * BLK)
-        parts.extend([up, up, low, low])
-    full = jnp.concatenate(parts, axis=1)
-    high = lax.reduce_precision(full, exponent_bits=8, mantissa_bits=7)
-    return jnp.concatenate([high, full - high], axis=0).astype(jnp.bfloat16)
+        ahead.extend(both(own(offsets[k, 0], offsets[k, 1])))
+        mirror.extend(both(jnp.transpose(own(offsets[k, 1], offsets[k, 0]), (0, 2, 1))))
+    blocks = jnp.stack([jnp.concatenate(ahead, axis=1), jnp.concatenate(mirror, axis=1)])
+    offdiag = (pairs[:, 0] != pairs[:, 1]).astype(jnp.float32)
+    sign = 1.0 - 2.0 * (jnp.arange(blocks.shape[2]) // 128 % 2).astype(jnp.float32)
+    return blocks, offdiag[:, None] * sign[None, :]
 
 
 def on_plane(pairs, offsets, amplitudes, slabs):
     shard, depth = slabs.shape[2], slabs.shape[4]
     rows_loc, cols_loc = amplitudes.shape[1], amplitudes.shape[2]
-    weights = ladder_weights(pairs, offsets, amplitudes)
+    own_blocks, sides = ladder_blocks(pairs, offsets, amplitudes)
     natural = slabs.reshape(STEPS, 2, shard * BLK, depth)
     turned = jnp.swapaxes(slabs, 2, 3)
     bf16, f32 = jnp.bfloat16, jnp.float32
@@ -281,13 +325,18 @@
             jax.ShapeDtypeStruct((4, P_SIZE * rows_loc, LANES), f32),
             jax.ShapeDtypeStruct((4, P_SIZE * rows_loc, LANES), f32),
         ),
-        in_specs=[pl.BlockSpec(memory_space=pltpu.VMEM), anywhere, anywhere],
+        in_specs=[pl.BlockSpec(memory_space=pltpu.VMEM)] * 2 + [anywhere, anywhere],
         out_specs=(anywhere, anywhere, anywhere),
         scratch_shapes=[
             pltpu.VMEM((STEPS, 2, rows_loc * BLK, depth), bf16),
             pltpu.VMEM((STEPS, 2, BLK, LANES, depth), bf16),
             pltpu.VMEM((rows_loc, STEPS * 256, LANES), bf16),
             pltpu.VMEM((4, P_SIZE * rows_loc, LANES), f32),
+            pltpu.VMEM((2 * P_SIZE, STEPS * 256), bf16),
+            pltpu.VMEM((6, 2, P_SIZE, STEPS * 256), bf16),
+            pltpu.VMEM((5, 2, P_SIZE, STEPS * 256), bf16),
+            pltpu.VMEM((P_SIZE // 2 * rows_loc, LANES), f32),
+            dma((5,)), dma((5,)),
             dma((7,)), dma((7,)), dma((7,)), dma((7,)), dma((8, 2)), dma((8, 2)),
             dma, dma, dma((4,)), dma((4,)), dma((2,)), dma((2, 2, 2)), dma((4,)),
         ],
@@ -295,7 +344,7 @@
             collective_id=0, has_side_effects=True, vmem_limit_bytes=60 * 1024 * 1024
         ),
         name="ladder_ring",
-    )(weights, natural, turned)
+    )(own_blocks, sides, natural, turned)
     row = lax.axis_index("vrow")
     col = lax.axis_index("vcol")
     chip = jnp.arange(4, dtype=jnp.int32)
@@ -307,12 +356,15 @@
     table = jnp.concatenate([block, half, col[None].astype(jnp.int32)])
     chunk = 16
     source = pl.BlockSpec((1, chunk, rows_loc, LANES), lambda i, j, t: (t[i], j, 0, 0))
+    other = pl.BlockSpec(
+        (1, chunk, rows_loc, LANES), lambda i, j, t: (t[i], jnp.where(t[i] == 3, j % 2, j), 0, 0)
+    )
     return pl.pallas_call(
         place_kernel,
         grid_spec=pltpu.PrefetchScalarGridSpec(
             num_scalar_prefetch=1,
             grid=(4, P_SIZE // chunk),
-            in_specs=[source, source],
+            in_specs=[source, other],
             out_specs=pl.BlockSpec((chunk, rows_loc, LANES), lambda i, j, t: (j, 0, i)),
         ),
         out_shape=jax.ShapeDtypeStruct((P_SIZE, rows_loc, cols_loc), f32),

time: 533 us -> 496 us (0.931)
  blocking collectives: 40.4 us -> 0 us
    psum x1 -> x0, blocking collectives: 40.4 us -> none  [broadcast(): return lax.psum(block, axis)]
where the time goes in v2:
time: 496 us; the launch traced here: 494 us
  Pallas kernels  469 us (95%)
  local copies, waits for them, and re-layouts  12.8 us (3%)
  between operations  10 us (2%)
    pallas_call x1, Pallas kernels, on_plane(): pl.pallas_call(ring_kernel, out_shape=(jax.ShapeDtypeStruct((8, 2, STEPS,...  449 us
    pallas_call x1, Pallas kernels, on_plane(): pl.pallas_call(place_kernel, grid_spec=pltpu.PrefetchScalarGridSpec(num_s...  19.8 us

profile of v2, /device:TPU:9, one launch (start us, length us, event | category | flops | bytes accessed | tf_op | source)
XLA Modules:
  0.0 494.4 jit_solution(5942918660625583012)
XLA Ops:
  0.0 0.8 fusion.10
  0.8 1.4 fusion.13
  12.1 1.3 gather_fusion.1
  13.4 1.3 gather_fusion
  14.7 0.6 pad_add_fusion.table
  15.3 0.7 broadcast_multiply_fusion.sides
  16.1 1.7 constant_dynamic-slice_fusion.2
  17.8 0.1 copy.38
  17.9 0.1 copy.39
  18.0 0.1 copy.37
  18.2 0.1 copy.40
  18.3 0.1 copy.32
  18.4 0.1 copy.34
  18.6 0.1 copy.18
  18.7 0.1 copy.16
  18.8 0.1 copy.28
  18.9 0.1 copy.30
  19.0 0.1 concatenate.11
  19.2 0.1 copy.22
  19.3 0.1 copy.20
  19.4 0.1 concatenate.10
  19.5 0.7 pad_maximum_fusion.own_blocks
  20.2 5.6 %copy.46 = bf16[2,2,32,8,2304]{4,2,3,1,0:T(8,128)(2,1)} copy(bf16[2,2,32,8,2304]{4,3,2,1,0:T(8,128)(2,1)} %param.9) | data formatting | bytes 9437184 | tf_op args[3]
  25.7 448.8 %ladder_ring.1 = (bf16[8,2,2,2,8,32,2304]{6,5,4,3,2,1,0:T(8,128)(2,1)}, f32[4,4096,128]{2,1,0:T(8,128)}, f32[4,4096,128]{2,1,0:T(8,128)}) custom-call(bf16[2,64,512]{2,1,0:T(8,128)(2,1)} %pad_maximum_fusion.own_blocks, f32[64,512]{1,0:T(8,128)} %broadcast_multiply_fusion.sides, bf16[2,2,256,2304]{3,2,1,0:T(8,128)(2,1)} %bitcast.45, ...), custom_call_target="tpu_custom_call" | custom-call | tf_op jit(solution)/shard_map/ladder_ring/pallas_call | solution.py:321
  474.5 19.8 %ladder_place.1 = f32[64,64,512]{2,1,0:T(8,128)} custom-call(s32[9]{0:T(128)} %pad_add_fusion.table, f32[4,64,64,128]{3,2,1,0:T(8,128)} %bitcast.47, f32[4,64,64,128]{3,2,1,0:T(8,128)} %bitcast.48), custom_call_target="tpu_custom_call" | custom-call | tf_op jit(solution)/shard_map/ladder_place/pallas_call | solution.py:362
  (15 shorter events, 0.1 us)

commit v3 on v2

--- a/solution.py
+++ b/solution.py
@@ -111,7 +111,7 @@
 
 
 def ring_kernel(
-    own_blocks, sides, natural, turned, gathered, mine, theirs,
+    own_blocks, sides, natural, turned, gathered, mine, theirs, late,
     rows, piece, factor, totals, weights, sums, came, packed, x_send, x_recv,
     f_send, f_recv, b_send, b_recv, s_send, s_recv, a_send, a_recv, o_send, o_recv, l_sem, p_sem, t_sem,
 ):
@@ -155,6 +155,8 @@
     a_own = pltpu.make_async_copy(natural, rows.at[:, :, pl.ds(col * width, width), :], l_sem.at[0])
     own = pltpu.make_async_copy(turned, gathered.at[0, core], l_sem.at[1])
 
+    forward[0].start()
+    backward[0].start()
     sums[0] = own_blocks[...]
     for i, other in enumerate(flips):
         swap = remote(sums.at[i], came.at[i], x_send.at[i], x_recv.at[i], other)
@@ -162,9 +164,8 @@
         swap.wait()
         sums[i + 1] = sums[i] + came[i]
 
-    for i in range(2):
-        forward[i].start()
-        backward[i].start()
+    forward[1].start()
+    backward[1].start()
     a_copy.start()
     own.start()
     a_own.start()
@@ -179,57 +180,58 @@
     weights[P_SIZE:] = (full - high.astype(jnp.float32)).astype(jnp.bfloat16)
 
     outs = [remote(totals.at[u], theirs.at[u], o_send.at[u], o_recv.at[u], partner) for u in range(3)]
-    outs.append(remote(packed, theirs.at[3, pl.ds(0, packed.shape[0])], o_send.at[3], o_recv.at[3], partner))
+    for h in range(2):
+        outs.append(remote(packed.at[h], late.at[h], o_send.at[3 + h], o_recv.at[3 + h], partner))
     send_last = row // 8 == col
     keeps = [pltpu.make_async_copy(totals.at[u], mine.at[u], t_sem.at[u]) for u in range(4)]
     count = rows.shape[2] // BLK
     shard = turned.shape[3]
 
-    def compute(u):
+    def loads_of(u):
         loads = []
         for e, slot in enumerate(PAIRS[u]):
             for c in range(2):
                 for k in range(2):
                     dst = piece.at[k, :, :, pl.ds((e * 2 + c) * shard, shard), :]
                     loads.append(pltpu.make_async_copy(gathered.at[slot, c, k], dst, p_sem.at[e, c, k]))
-        for load in loads:
-            load.start()
-        for load in loads:
-            load.wait()
-
-        def products(i, carry):
+        return loads
+
+    def compute(u, parts):
+        part_rows = count // parts
+
+        def products(h, i, carry):
             k = i // 8
             t = lax.rem(i // 4, 2)
             d = lax.rem(i, 4)
             cols = piece[k, 1 - t, pl.ds(d * 2, 2)].reshape(2 * LANES, piece.shape[-1])
             part = lax.dot_general(
-                rows[k, t], cols, (((1,), (1,)), ((), ())), preferred_element_type=jnp.float32
-            ).reshape(count, BLK, 2 * LANES)
+                rows[k, t, pl.ds(h * part_rows * BLK, part_rows * BLK)], cols, (((1,), (1,)), ((), ())), preferred_element_type=jnp.float32
+            ).reshape(part_rows, BLK, 2 * LANES)
             part = jnp.concatenate([part[:, :, :LANES], part[:, :, LANES:]], axis=1)
             high = part.astype(jnp.bfloat16)
             low = (part - high.astype(jnp.float32)).astype(jnp.bfloat16)
             at = k * 256 + t * 128 + d * 16
-            factor[:, pl.ds(pl.multiple_of(at, 16), 16), :] = high
-            factor[:, pl.ds(pl.multiple_of(at + 64, 16), 16), :] = low
+            factor[:part_rows, pl.ds(pl.multiple_of(at, 16), 16), :] = high
+            factor[:part_rows, pl.ds(pl.multiple_of(at + 64, 16), 16), :] = low
             return carry
 
-        lax.fori_loop(0, 16, products, 0)
-
-        def contract(a, carry):
+        def contract(h, a, carry):
             res = jnp.dot(weights[...], factor[a], preferred_element_type=jnp.float32)
             res = res[:P_SIZE] + res[P_SIZE:]
-            totals[u, pl.ds(a, P_SIZE, stride=count), :] = res
+            totals[u, pl.ds(h * part_rows + a, P_SIZE, stride=count), :] = res
             if u == 3:
                 moved = pltpu.roll(res, 64, 1)
                 half = P_SIZE // 2
                 low = lax.broadcasted_iota(jnp.int32, (half, LANES), 1) < 64
                 opposite = jnp.where(low, moved[:half], res[half:])
                 near = jnp.where(low, res[:half], moved[half:])
-                packed[pl.ds(a, half, stride=count), :] = jnp.where(send_last, opposite, near)
+                packed[h, pl.ds(a, half, stride=part_rows), :] = jnp.where(send_last, opposite, near)
             return carry
 
-        lax.fori_loop(0, count, contract, 0)
-        outs[u].start()
+        for h in range(parts):
+            lax.fori_loop(0, 16, functools.partial(products, h), 0)
+            lax.fori_loop(0, part_rows, functools.partial(contract, h), 0)
+            outs[u + h].start()
         keeps[u].start()
 
     def sibling_here(slots):
@@ -254,31 +256,52 @@
         if i in (1, 3, 5):
             u = i // 2
             sibling_here(PAIRS[u])
-            compute(u)
-    own.wait()
-    sibling_here(PAIRS[3])
-    compute(3)
+            loads = loads_of(u)
+            for load in loads:
+                load.start()
+            for load in loads:
+                load.wait()
+            compute(u, 1)
+        if i == 5:
+            own.wait()
+            sibling_here((0,))
+            loads = loads_of(3)
+            for load in loads[:4]:
+                load.start()
+    sibling_here((7,))
+    for load in loads[4:]:
+        load.start()
+    for load in loads:
+        load.wait()
+    compute(3, 2)
     for copy in forward + backward + list(shares.values()) + [a_copy]:
         copy.wait_send()
-    for u in range(4):
-        keeps[u].wait()
-        outs[u].wait()
-
-
-def place_kernel(table, mine, theirs, out):
+    for copy in keeps + outs:
+        copy.wait()
+
+
+def place_kernel(table, mine, theirs, late, out):
     i = pl.program_id(0)
+    last = table[i] == 3
     half = table[4 + i]
-    other_half = jnp.where(table[i] == 3, pl.program_id(1) // 2, half)
+    other_half = jnp.where(last, pl.program_id(1) // 2, half)
     swap = table[8]
-    a = mine[0]
-    b = theirs[0]
-    a = jnp.where(half == 0, a[:, :, :64], a[:, :, 64:])
-    b = jnp.where(other_half == 0, b[:, :, :64], b[:, :, 64:])
-    first = jnp.where(swap == 0, a, b)
-    second = jnp.where(swap == 0, b, a)
-    out[...] = jnp.concatenate(
-        [first[:, :, :32], second[:, :, :32], first[:, :, 32:], second[:, :, 32:]], axis=-1
-    )
+    shape = out.shape
+    a = mine[0].reshape(-1, LANES)
+    b = jnp.where(last, jnp.concatenate([late[0], late[1]], axis=1), theirs[0]).reshape(-1, LANES)
+    lane = lax.broadcasted_iota(jnp.int32, a.shape, 1)
+
+    def spread(x, source, target):
+        shift = target - source + LANES
+        return jnp.where(
+            lane < 64,
+            pltpu.roll(x, lax.rem(shift, LANES), 1),
+            pltpu.roll(x, lax.rem(shift + 32, LANES), 1),
+        )
+
+    a = spread(a, half * 64, swap * 32)
+    b = spread(b, other_half * 64, 32 - swap * 32)
+    out[...] = jnp.where(lane // 32 % 2 == swap, a, b).reshape(shape)
 
 
 def ladder_blocks(pairs, offsets, amplitudes):
@@ -318,15 +341,16 @@
     bf16, f32 = jnp.bfloat16, jnp.float32
     dma = pltpu.SemaphoreType.DMA
     anywhere = pl.BlockSpec(memory_space=pl.ANY)
-    _, mine, theirs = pl.pallas_call(
+    _, mine, theirs, late = pl.pallas_call(
         ring_kernel,
         out_shape=(
             jax.ShapeDtypeStruct((8, 2, STEPS, 2, BLK, shard, depth), bf16),
             jax.ShapeDtypeStruct((4, P_SIZE * rows_loc, LANES), f32),
             jax.ShapeDtypeStruct((4, P_SIZE * rows_loc, LANES), f32),
+            jax.ShapeDtypeStruct((2, P_SIZE // 2 * rows_loc // 2, LANES), f32),
         ),
         in_specs=[pl.BlockSpec(memory_space=pltpu.VMEM)] * 2 + [anywhere, anywhere],
-        out_specs=(anywhere, anywhere, anywhere),
+        out_specs=(anywhere,) * 4,
         scratch_shapes=[
             pltpu.VMEM((STEPS, 2, rows_loc * BLK, depth), bf16),
             pltpu.VMEM((STEPS, 2, BLK, LANES, depth), bf16),
@@ -335,10 +359,10 @@
             pltpu.VMEM((2 * P_SIZE, STEPS * 256), bf16),
             pltpu.VMEM((6, 2, P_SIZE, STEPS * 256), bf16),
             pltpu.VMEM((5, 2, P_SIZE, STEPS * 256), bf16),
-            pltpu.VMEM((P_SIZE // 2 * rows_loc, LANES), f32),
+            pltpu.VMEM((2, P_SIZE // 2 * rows_loc // 2, LANES), f32),
             dma((5,)), dma((5,)),
             dma((7,)), dma((7,)), dma((7,)), dma((7,)), dma((8, 2)), dma((8, 2)),
-            dma, dma, dma((4,)), dma((4,)), dma((2,)), dma((2, 2, 2)), dma((4,)),
+            dma, dma, dma((5,)), dma((5,)), dma((2,)), dma((2, 2, 2)), dma((4,)),
         ],
         compiler_params=pltpu.CompilerParams(
             collective_id=0, has_side_effects=True, vmem_limit_bytes=60 * 1024 * 1024
@@ -357,19 +381,27 @@
     chunk = 16
     source = pl.BlockSpec((1, chunk, rows_loc, LANES), lambda i, j, t: (t[i], j, 0, 0))
     other = pl.BlockSpec(
-        (1, chunk, rows_loc, LANES), lambda i, j, t: (t[i], jnp.where(t[i] == 3, j % 2, j), 0, 0)
+        (1, chunk, rows_loc, LANES), lambda i, j, t: (t[i], jnp.where(t[i] == 3, 0, j), 0, 0)
+    )
+    final = pl.BlockSpec(
+        (2, chunk, rows_loc // 2, LANES), lambda i, j, t: (0, jnp.where(t[i] == 3, j % 2, 0), 0, 0)
     )
     return pl.pallas_call(
         place_kernel,
         grid_spec=pltpu.PrefetchScalarGridSpec(
             num_scalar_prefetch=1,
             grid=(4, P_SIZE // chunk),
-            in_specs=[source, other],
+            in_specs=[source, other, final],
             out_specs=pl.BlockSpec((chunk, rows_loc, LANES), lambda i, j, t: (j, 0, i)),
         ),
         out_shape=jax.ShapeDtypeStruct((P_SIZE, rows_loc, cols_loc), f32),
         name="ladder_place",
-    )(table, mine.reshape(4, P_SIZE, rows_loc, LANES), theirs.reshape(4, P_SIZE, rows_loc, LANES))
+    )(
+        table,
+        mine.reshape(4, P_SIZE, rows_loc, LANES),
+        theirs.reshape(4, P_SIZE, rows_loc, LANES),
+        late.reshape(2, P_SIZE // 2, rows_loc // 2, LANES),
+    )
 
 
 def solution(mesh):

time: 496 us -> 478 us (0.964)
  Pallas kernels: 469 us -> 452 us
    pallas_call x1, Pallas kernels: 449 us -> 433 us  [on_plane(): pl.pallas_call(ring_kernel, out_shape=(jax.ShapeDtypeStruct((8, 2, STEPS,...]
where the time goes in v3:
time: 478 us
  Pallas kernels  452 us (95%)
  local copies, waits for them, and re-layouts  12.9 us (3%)
  between operations  10 us (2%)
    pallas_call x1, Pallas kernels, on_plane(): pl.pallas_call(ring_kernel, out_shape=(jax.ShapeDtypeStruct((8, 2, STEPS,...  433 us
    pallas_call x1, Pallas kernels, on_plane(): pl.pallas_call(place_kernel, grid_spec=pltpu.PrefetchScalarGridSpec(num_s...  18.9 us

profile of v3, /device:TPU:9, one launch (start us, length us, event | category | flops | bytes accessed | tf_op | source)
XLA Modules:
  0.0 477.6 jit_solution(2082916630042153320)
XLA Ops:
  0.0 0.8 fusion.10
  0.8 1.4 fusion.13
  12.1 1.3 gather_fusion.1
  13.4 1.3 gather_fusion
  14.7 0.7 pad_add_fusion.table
  15.4 0.7 broadcast_multiply_fusion.sides
  16.1 1.7 constant_dynamic-slice_fusion.2
  17.8 0.1 copy.38
  18.0 0.1 copy.39
  18.1 0.1 copy.37
  18.3 0.1 copy.40
  18.4 0.1 copy.32
  18.5 0.1 copy.34
  18.7 0.1 copy.18
  18.8 0.1 copy.16
  18.9 0.1 copy.28
  19.0 0.1 copy.30
  19.1 0.1 concatenate.11
  19.3 0.1 copy.22
  19.3 0.1 copy.20
  19.5 0.1 concatenate.10
  19.6 0.7 pad_maximum_fusion.own_blocks
  20.2 5.6 %copy.46 = bf16[2,2,32,8,2304]{4,2,3,1,0:T(8,128)(2,1)} copy(bf16[2,2,32,8,2304]{4,3,2,1,0:T(8,128)(2,1)} %param.9) | data formatting | bytes 9437184 | tf_op args[3]
  25.8 432.9 %ladder_ring.1 = (bf16[8,2,2,2,8,32,2304]{6,5,4,3,2,1,0:T(8,128)(2,1)}, f32[4,4096,128]{2,1,0:T(8,128)}, f32[4,4096,128]{2,1,0:T(8,128)}, f32[2,1024,128]{2,1,0:T(8,128)}) custom-call(bf16[2,64,512]{2,1,0:T(8,128)(2,1)} %pad_maximum_fusion.own_blocks, f32[64,512]{1,0:T(8,128)} %broadcast_multiply_fusion.sides, bf16[2,2,256,2304]{3,2,1,0:T(8,128)(2,1)} %bitcast.46, ...), custom_call_target="tpu_custom_call" | custom-call | tf_op jit(solution)/shard_map/ladder_ring/pallas_call | solution.py:344
  458.7 18.9 %ladder_place.1 = f32[64,64,512]{2,1,0:T(8,128)} custom-call(s32[9]{0:T(128)} %pad_add_fusion.table, f32[4,64,64,128]{3,2,1,0:T(8,128)} %bitcast.48, f32[4,64,64,128]{3,2,1,0:T(8,128)} %bitcast.49, f32[2,32,32,128]{3,2,1,0:T(8,128)} %bitcast.50), custom_call_target="tpu_custom_call" | custom-call | tf_op jit(solution)/shard_map/ladder_place/pallas_call | solution.py:389
  (15 shorter events, 0.1 us)

commit v4 on v3

--- a/solution.py
+++ b/solution.py
@@ -230,7 +230,7 @@
 
         for h in range(parts):
             lax.fori_loop(0, 16, functools.partial(products, h), 0)
-            lax.fori_loop(0, part_rows, functools.partial(contract, h), 0)
+            lax.fori_loop(0, part_rows, functools.partial(contract, h), 0, unroll=4)
             outs[u + h].start()
         keeps[u].start()
 
@@ -280,16 +280,13 @@
         copy.wait()
 
 
-def place_kernel(table, mine, theirs, late, out):
-    i = pl.program_id(0)
-    last = table[i] == 3
-    half = table[4 + i]
-    other_half = jnp.where(last, pl.program_id(1) // 2, half)
+def place_kernel(table, *refs):
+    mine, theirs, late, out = refs[:4], refs[4:8], refs[8], refs[9]
+    chunk, rows_loc = out.shape[:2]
+    step = pl.program_id(0)
     swap = table[8]
-    shape = out.shape
-    a = mine[0].reshape(-1, LANES)
-    b = jnp.where(last, jnp.concatenate([late[0], late[1]], axis=1), theirs[0]).reshape(-1, LANES)
-    lane = lax.broadcasted_iota(jnp.int32, a.shape, 1)
+    lane = lax.broadcasted_iota(jnp.int32, (chunk * rows_loc, LANES), 1)
+    late_block = jnp.concatenate([late[0], late[1]], axis=1).reshape(-1, LANES)
 
     def spread(x, source, target):
         shift = target - source + LANES
@@ -299,9 +296,16 @@
             pltpu.roll(x, lax.rem(shift + 32, LANES), 1),
         )
 
-    a = spread(a, half * 64, swap * 32)
-    b = spread(b, other_half * 64, 32 - swap * 32)
-    out[...] = jnp.where(lane // 32 % 2 == swap, a, b).reshape(shape)
+    for i in range(4):
+        last = table[i] == 3
+        half = table[4 + i]
+        other_half = jnp.where(last, step // (P_SIZE // chunk // 2), half)
+        a = mine[i][0].reshape(-1, LANES)
+        b = jnp.where(last, late_block, theirs[i][0].reshape(-1, LANES))
+        a = spread(a, half * 64, swap * 32)
+        b = spread(b, other_half * 64, 32 - swap * 32)
+        block = jnp.where(lane // 32 % 2 == swap, a, b)
+        out[:, :, i * LANES : (i + 1) * LANES] = block.reshape(chunk, rows_loc, LANES)
 
 
 def ladder_blocks(pairs, offsets, amplitudes):
@@ -378,30 +382,32 @@
     block = jnp.array([3, 0, 1, 2, 3, 2, 1, 0], jnp.int32)[rel]
     half = jnp.array([0, 1, 1, 1, 1, 0, 0, 0], jnp.int32)[rel]
     table = jnp.concatenate([block, half, col[None].astype(jnp.int32)])
-    chunk = 16
-    source = pl.BlockSpec((1, chunk, rows_loc, LANES), lambda i, j, t: (t[i], j, 0, 0))
-    other = pl.BlockSpec(
-        (1, chunk, rows_loc, LANES), lambda i, j, t: (t[i], jnp.where(t[i] == 3, 0, j), 0, 0)
-    )
-    final = pl.BlockSpec(
-        (2, chunk, rows_loc // 2, LANES), lambda i, j, t: (0, jnp.where(t[i] == 3, j % 2, 0), 0, 0)
-    )
+    chunk = 8
+    steps = P_SIZE // chunk
+    shape = (1, chunk, rows_loc, LANES)
+
+    def from_mine(i):
+        return pl.BlockSpec(shape, lambda j, t: (t[i], j, 0, 0))
+
+    def from_theirs(i):
+        return pl.BlockSpec(shape, lambda j, t: (t[i], jnp.where(t[i] == 3, 0, j), 0, 0))
+
+    final = pl.BlockSpec((2, chunk, rows_loc // 2, LANES), lambda j, t: (0, lax.rem(j, steps // 2), 0, 0))
+    mine = mine.reshape(4, P_SIZE, rows_loc, LANES)
+    theirs = theirs.reshape(4, P_SIZE, rows_loc, LANES)
+    late = late.reshape(2, P_SIZE // 2, rows_loc // 2, LANES)
     return pl.pallas_call(
         place_kernel,
         grid_spec=pltpu.PrefetchScalarGridSpec(
             num_scalar_prefetch=1,
-            grid=(4, P_SIZE // chunk),
-            in_specs=[source, other, final],
-            out_specs=pl.BlockSpec((chunk, rows_loc, LANES), lambda i, j, t: (j, 0, i)),
+            grid=(steps,),
+            in_specs=[from_mine(i) for i in range(4)] + [from_theirs(i) for i in range(4)] + [final],
+            out_specs=pl.BlockSpec((chunk, rows_loc, cols_loc), lambda j, t: (j, 0, 0)),
         ),
         out_shape=jax.ShapeDtypeStruct((P_SIZE, rows_loc, cols_loc), f32),
+        compiler_params=pltpu.CompilerParams(vmem_limit_bytes=32 * 1024 * 1024),
         name="ladder_place",
-    )(
-        table,
-        mine.reshape(4, P_SIZE, rows_loc, LANES),
-        theirs.reshape(4, P_SIZE, rows_loc, LANES),
-        late.reshape(2, P_SIZE // 2, rows_loc // 2, LANES),
-    )
+    )(table, *[mine] * 4, *[theirs] * 4, late)
 
 
 def solution(mesh):

time: 478 us -> 471 us (0.985)
  Pallas kernels: 452 us -> 437 us
  local copies, waits for them, and re-layouts: 12.9 us -> 21 us
    unnamed x5 -> x11, local copies, waits for them, and re-layouts: 6.12 us -> 14.1 us
    pallas_call x1, Pallas kernels: 18.9 us -> 11.1 us  [on_plane(): pl.pallas_call(place_kernel, grid_spec=pltpu.PrefetchScalarGridSpec(num_s...]
    pallas_call x1, Pallas kernels: 433 us -> 426 us  [on_plane(): pl.pallas_call(ring_kernel, out_shape=(jax.ShapeDtypeStruct((8, 2, STEPS,...]
where the time goes in v4:
time: 471 us; the launch traced here: 470 us
  Pallas kernels  437 us (93%)
  local copies, waits for them, and re-layouts  21 us (4%)
  between operations  10.3 us (2%)
    pallas_call x1, Pallas kernels, on_plane(): pl.pallas_call(ring_kernel, out_shape=(jax.ShapeDtypeStruct((8, 2, STEPS,...  426 us
    unnamed x11, local copies, waits for them, and re-layouts  14.1 us
    pallas_call x1, Pallas kernels, on_plane(): pl.pallas_call(place_kernel, grid_spec=pltpu.PrefetchScalarGridSpec(num_s...  11.1 us

profile of v4, /device:TPU:9, one launch (start us, length us, event | category | flops | bytes accessed | tf_op | source)
XLA Modules:
  0.0 470.3 jit_solution(531551198025841493)
XLA Ops:
  0.0 0.8 fusion.10
  0.8 1.5 fusion.13
  12.5 1.3 gather_fusion.1
  13.8 1.3 gather_fusion
  15.1 0.1 pad_add_fusion.table
  15.1 0.7 broadcast_multiply_fusion.sides
  15.9 1.8 constant_dynamic-slice_fusion.2
  17.7 0.1 copy.38
  17.8 0.1 copy.39
  17.9 0.1 copy.37
  18.1 0.1 copy.40
  18.2 0.1 copy.32
  18.3 0.1 copy.34
  18.5 0.1 copy.18
  18.6 0.1 copy.16
  18.7 0.1 copy.28
  18.8 0.1 copy.30
  18.9 0.1 concatenate.11
  19.1 0.1 copy.22
  19.2 0.1 copy.20
  19.3 0.1 concatenate.10
  19.4 0.7 pad_maximum_fusion.own_blocks
  20.1 5.6 %copy.46 = bf16[2,2,32,8,2304]{4,2,3,1,0:T(8,128)(2,1)} copy(bf16[2,2,32,8,2304]{4,3,2,1,0:T(8,128)(2,1)} %param.9) | data formatting | bytes 9437184 | tf_op args[3]
  25.6 425.6 %ladder_ring.1 = (bf16[8,2,2,2,8,32,2304]{6,5,4,3,2,1,0:T(8,128)(2,1)}, f32[4,4096,128]{2,1,0:T(8,128)}, f32[4,4096,128]{2,1,0:T(8,128)}, f32[2,1024,128]{2,1,0:T(8,128)}) custom-call(bf16[2,64,512]{2,1,0:T(8,128)(2,1)} %pad_maximum_fusion.own_blocks, f32[64,512]{1,0:T(8,128)} %broadcast_multiply_fusion.sides, bf16[2,2,256,2304]{3,2,1,0:T(8,128)(2,1)} %bitcast.55, ...), custom_call_target="tpu_custom_call" | custom-call | tf_op jit(solution)/shard_map/ladder_ring/pallas_call | solution.py:348
  451.2 0.0 copy-start
  451.2 3.4 copy-done
  454.6 0.0 copy-start.1
  454.6 3.4 copy-done.1
  458.0 0.0 copy-start.2
  458.0 1.2 copy-done.2
  459.2 11.1 %ladder_place.1 = f32[64,64,512]{2,1,0:T(8,128)} custom-call(s32[9]{0:T(128)S(1)} %pad_add_fusion.table, f32[4,64,64,128]{3,2,1,0:T(8,128)S(1)} %bitcast.46, f32[4,64,64,128]{3,2,1,0:T(8,128)S(1)} %bitcast.47, f32[4,64,64,128]{3,2,1,0:T(8,128)S(1)} %bitcast.48, f32[4,64,64,128]{3,2,1,0:T(8,128)S(1)} %bitcast.49, f32[4,64,64,128]{3,2,1,0:T(8,128)S(1)} %bitcast.50, ...), custom_call_target="tpu_custom_call" | custom-call | tf_op jit(solution)/shard_map/ladder_place/pallas_call | solution.py:399
  (15 shorter events, 0.1 us)
Async XLA Ops:
  451.2 3.4 copy-start
  454.6 3.4 copy-start.1
  458.0 1.2 copy-start.2

commit v5 on v4

--- a/solution.py
+++ b/solution.py
@@ -229,8 +229,8 @@
             return carry
 
         for h in range(parts):
-            lax.fori_loop(0, 16, functools.partial(products, h), 0)
-            lax.fori_loop(0, part_rows, functools.partial(contract, h), 0, unroll=4)
+            lax.fori_loop(0, 16, functools.partial(products, h), 0, unroll=2)
+            lax.fori_loop(0, part_rows, functools.partial(contract, h), 0, unroll=8)
             outs[u + h].start()
         keeps[u].start()
 

time: 471 us -> 468 us (level)
  no operation moved by 1% of the time
where the time goes in v5:
time: 468 us
  Pallas kernels  434 us (93%)
  local copies, waits for them, and re-layouts  20.8 us (4%)
  between operations  10.3 us (2%)
    pallas_call x1, Pallas kernels, on_plane(): pl.pallas_call(ring_kernel, out_shape=(jax.ShapeDtypeStruct((8, 2, STEPS,...  423 us
    unnamed x11, local copies, waits for them, and re-layouts  14.1 us
    pallas_call x1, Pallas kernels, on_plane(): pl.pallas_call(place_kernel, grid_spec=pltpu.PrefetchScalarGridSpec(num_s...  11.1 us

profile of v5, /device:TPU:9, one launch (start us, length us, event | category | flops | bytes accessed | tf_op | source)
XLA Modules:
  0.0 467.6 jit_solution(15004995566521059406)
XLA Ops:
  0.0 0.8 fusion.10
  0.8 1.5 fusion.13
  12.5 1.3 gather_fusion.1
  13.8 1.3 gather_fusion
  15.1 0.1 pad_add_fusion.table
  15.1 0.7 broadcast_multiply_fusion.sides
  15.9 1.6 constant_dynamic-slice_fusion.2
  17.5 0.1 copy.38
  17.6 0.1 copy.39
  17.8 0.1 copy.37
  17.9 0.1 copy.40
  18.1 0.1 copy.32
  18.2 0.1 copy.34
  18.3 0.1 copy.18
  18.4 0.1 copy.16
  18.6 0.1 copy.28
  18.7 0.1 copy.30
  18.8 0.1 concatenate.11
  18.9 0.1 copy.22
  19.0 0.1 copy.20
  19.1 0.1 concatenate.10
  19.2 0.7 pad_maximum_fusion.own_blocks
  19.9 5.6 %copy.46 = bf16[2,2,32,8,2304]{4,2,3,1,0:T(8,128)(2,1)} copy(bf16[2,2,32,8,2304]{4,3,2,1,0:T(8,128)(2,1)} %param.9) | data formatting | bytes 9437184 | tf_op args[3]
  25.5 422.9 %ladder_ring.1 = (bf16[8,2,2,2,8,32,2304]{6,5,4,3,2,1,0:T(8,128)(2,1)}, f32[4,4096,128]{2,1,0:T(8,128)}, f32[4,4096,128]{2,1,0:T(8,128)}, f32[2,1024,128]{2,1,0:T(8,128)}) custom-call(bf16[2,64,512]{2,1,0:T(8,128)(2,1)} %pad_maximum_fusion.own_blocks, f32[64,512]{1,0:T(8,128)} %broadcast_multiply_fusion.sides, bf16[2,2,256,2304]{3,2,1,0:T(8,128)(2,1)} %bitcast.55, ...), custom_call_target="tpu_custom_call" | custom-call | tf_op jit(solution)/shard_map/ladder_ring/pallas_call | solution.py:348
  448.4 0.0 copy-start
  448.4 3.4 copy-done
  451.8 0.0 copy-start.1
  451.8 3.4 copy-done.1
  455.2 0.0 copy-start.2
  455.2 1.2 copy-done.2
  456.4 11.1 %ladder_place.1 = f32[64,64,512]{2,1,0:T(8,128)} custom-call(s32[9]{0:T(128)S(1)} %pad_add_fusion.table, f32[4,64,64,128]{3,2,1,0:T(8,128)S(1)} %bitcast.46, f32[4,64,64,128]{3,2,1,0:T(8,128)S(1)} %bitcast.47, f32[4,64,64,128]{3,2,1,0:T(8,128)S(1)} %bitcast.48, f32[4,64,64,128]{3,2,1,0:T(8,128)S(1)} %bitcast.49, f32[4,64,64,128]{3,2,1,0:T(8,128)S(1)} %bitcast.50, ...), custom_call_target="tpu_custom_call" | custom-call | tf_op jit(solution)/shard_map/ladder_place/pallas_call | solution.py:399
  (15 shorter events, 0.1 us)
Async XLA Ops:
  448.4 3.4 copy-start
  451.8 3.4 copy-start.1
  455.2 1.2 copy-start.2
